TPU v7x, 512 devices: a whole 4x8x8 slice. The times are simulated.
512 devices in a mesh: dp: 16 (over z_lo, x), zero: 32 (over y, z_hi, core).
Axes of the slice: x: 4, y: 8, z: 8 (z_hi: 2, z_lo: 4; z = z_hi * 4 + z_lo), core: 2. Of those that a mesh axis runs over, the one named last changes fastest.
Arguments:
- gate_up: bfloat16 [2, 4096, 14336], P(None, 'dp', 'zero'), may hold values from -6 to 6
- cot_mean: bfloat16 [4096, 4096], P('dp', 'zero'), may hold values from -6 to 6
- label_rows: bfloat16 [64, 4096], P(None, 'dp'), may hold values from -6 to 6
- true_labels: int32 [4096], P('dp'), may hold values from 0 to 63
- sampled_labels: int32 [4096], P('dp'), may hold values from 0 to 63
- weight: bfloat16 [14336, 4096], P('zero', 'dp'), may hold values from -4 to 4
- moment: bfloat16 [14336, 4096], P('zero', 'dp'), may hold values from -0.29882812 to 0.29882812
- curvature: bfloat16 [14336, 4096], P('zero', 'dp'), may hold values from 0.0099487305 to 1
- bits: int32 [14336, 4096], P('zero', 'dp'), may hold values from 0 to 16383
Outputs:
- new_weight: bfloat16 [14336, 4096], P('zero')
- new_moment: bfloat16 [14336, 4096], P('zero', 'dp')
- new_curvature: bfloat16 [14336, 4096], P('zero', 'dp')
All inputs are finite; a program needn't handle non-finite values.
Results may differ from a plain program's by a relative error of at most 0.014.
Values may be sent and summed in bfloat16 or wider, within the bound.
A program may use at most 64 MiB of HBM per device.

v0:
```python
import math

import jax
import jax.numpy as jnp
from jax import lax
from jax.sharding import PartitionSpec as P

beta_one = 0.965
beta_two = 0.99
gamma_rate = 0.5
learn_rate = 0.05
decay_rate = 0.1


def dither(value, noise):
    return (value * (1.0 + (noise - 0.5) / 8.0)).astype(jnp.bfloat16)


def on_device(
    gate_up, cot_mean, label_rows, true_labels, sampled_labels, weight, moment, curvature, bits
):
    tok_rows = gate_up.shape[1]
    cands = label_rows.shape[0]
    groups = lax.axis_size("dp")
    factor = 1.0 / math.sqrt(tok_rows * groups)
    gate_part = gate_up[0].astype(jnp.float32)
    up_part = gate_up[1].astype(jnp.float32)
    hidden = (jax.nn.silu(gate_part) * up_part).astype(jnp.bfloat16)
    classes = jnp.arange(cands, dtype=jnp.int32)
    hot_true = (true_labels[:, None] == classes[None, :]).astype(jnp.bfloat16)
    hot_sampled = (sampled_labels[:, None] == classes[None, :]).astype(jnp.bfloat16)
    label_part = jnp.dot(
        hidden.T,
        jnp.concatenate([hot_true, hot_sampled], axis=1),
        preferred_element_type=jnp.float32,
    )
    label_total = lax.psum(label_part.astype(jnp.bfloat16), "dp").astype(jnp.float32)
    terms = jnp.dot(
        hidden.T,
        lax.all_gather(cot_mean, "zero", axis=1, tiled=True),
        preferred_element_type=jnp.float32,
    )
    owned = lax.psum_scatter(
        terms.astype(jnp.bfloat16), "dp", scatter_dimension=1, tiled=True
    ).astype(jnp.float32)
    label_wide = label_rows.astype(jnp.float32)
    grad_true = (
        owned - jnp.dot(label_total[:, :cands], label_wide, precision=lax.Precision.HIGHEST)
    ) * factor
    grad_sampled = (
        owned - jnp.dot(label_total[:, cands:], label_wide, precision=lax.Precision.HIGHEST)
    ) * factor
    low_bits = bits % 128
    high_bits = bits // 128
    noise_one = (low_bits.astype(jnp.float32) + 0.5) / 128.0
    noise_two = (high_bits.astype(jnp.float32) + 0.5) / 128.0
    noise_three = (((3 * low_bits + 5 * high_bits) % 128).astype(jnp.float32) + 0.5) / 128.0
    new_moment = dither(
        beta_one * moment.astype(jnp.float32) + (1.0 - beta_one) * grad_true, noise_one
    )
    new_curvature = dither(
        beta_two * curvature.astype(jnp.float32) + (1.0 - beta_two) * grad_sampled * grad_sampled,
        noise_two,
    )
    ratio = jnp.clip(
        new_moment.astype(jnp.float32) / (gamma_rate * new_curvature.astype(jnp.float32)), -1.0, 1.0
    )
    shrunk = weight.astype(jnp.float32) * (1.0 - learn_rate * decay_rate) - learn_rate * ratio
    weight_piece = dither(shrunk, noise_three)
    new_weight = lax.all_gather(weight_piece, "dp", axis=1, tiled=True)
    return (new_weight, new_moment, new_curvature)


def solution(mesh):
    in_specs = (
        P(None, "dp", "zero"),
        P("dp", "zero"),
        P(None, "dp"),
        P("dp"),
        P("dp"),
        P("zero", "dp"),
        P("zero", "dp"),
        P("zero", "dp"),
        P("zero", "dp"),
    )
    out_specs = (P("zero", None), P("zero", "dp"), P("zero", "dp"))
    return jax.shard_map(
        on_device, mesh=mesh, in_specs=in_specs, out_specs=out_specs, check_vma=False
    )
```

profile of v0, /device:TPU:4, one launch (start us, length us, event | category | flops | bytes accessed | tf_op | source)
XLA Modules:
  0.0 387.3 jit_solution(16972792300468119694)
XLA Ops:
  8.0 0.0 copy-start
  8.0 0.0 all-gather.3.cloned.1.call-start
  8.1 0.7 all-gather.3.cloned.1.call-update
  8.7 0.0 all-reduce.2.cloned.1.call-start
  8.8 0.8 iota_compare_fusion
  9.6 1.2 fusion.17
  10.8 0.9 convolution_convert_fusion.1
  11.8 0.0 all-reduce.2.cloned.1.call-update
  11.8 0.0 copy-start.1
  11.8 0.0 copy-start.2
  11.8 0.0 reduce-scatter.2.cloned.1.call-start
  11.9 99.6 %all-gather.3.cloned.1.call-done = bf16[256,4096]{1,0:T(8,128)(2,1)} async-done(((bf16[256,128]{1,0:T(8,128)(2,1)}), bf16[256,4096]{1,0:T(8,128)(2,1)}) %all-gather.3.cloned.1.call-update) | async-done | bytes 2097168 | tf_op jit(solution)/shard_map/all_gather | solution.py:40
  111.4 4.6 %convolution_convert_fusion = bf16[448,4096]{1,0:T(8,128)(2,1)} fusion(bf16[256,448]{0,1:T(8,128)(2,1)S(1)} %fusion.17, bf16[256,4096]{1,0:T(8,128)(2,1)} %all-gather.3.cloned.1.call-done), kind=kOutput, calls=%fused_computation | convolution fusion | flops 941359104 | bytes 5996544 | tf_op jit(solution)/shard_map/dot_general | solution.py:38
  116.0 0.0 reduce-scatter.2.cloned.1.call-update
  116.0 0.0 all-gather.5.cloned.1.call-start
  116.1 67.2 %all-reduce.2.cloned.1.call-done = bf16[448,128]{1,0:T(8,128)(2,1)} async-done(((bf16[448,128]{1,0:T(8,128)(2,1)}), bf16[448,128]{1,0:T(8,128)(2,1)}) %all-reduce.2.cloned.1.call-update) | async-done | bytes 114704 | tf_op jit(solution)/shard_map/psum | solution.py:37
  183.2 96.9 %reduce-scatter.2.cloned.1.call-done = bf16[448,256]{1,0:T(8,128)(2,1)} async-done(((bf16[448,4096]{1,0:T(8,128)(2,1)}), bf16[448,256]{1,0:T(8,128)(2,1)}) %reduce-scatter.2.cloned.1.call-update) | async-done | bytes 229392 | tf_op jit(solution)/shard_map/reduce_scatter | solution.py:43
  280.2 1.4 fusion.3
  281.6 0.0 copy-done.3
  281.6 0.0 copy-start.5
  281.7 3.0 fusion.16
  284.7 0.0 all-gather.5.cloned.1.call-update
  284.7 90.7 %all-gather.5.cloned.1.call-done = bf16[448,4096]{1,0:T(8,128)(2,1)} async-done(((bf16[448,256]{1,0:T(8,128)(2,1)}), bf16[448,4096]{1,0:T(8,128)(2,1)}) %all-gather.5.cloned.1.call-update) | async-done | bytes 3670032 | tf_op jit(solution)/shard_map/all_gather | solution.py:70
  375.4 4.3 %copy.18 = bf16[448,4096]{1,0:T(8,128)(2,1)} copy(bf16[448,4096]{1,0:T(8,128)(2,1)} %all-gather.5.cloned.1.call-done) | data formatting | bytes 7340032
  (7 shorter events, 0.0 us)
Async XLA Ops:
  8.0 272.2 %copy-start = (bf16[64,256]{1,0:T(8,128)(2,1)S(1)}, bf16[64,256]{1,0:T(8,128)(2,1)}, u32[]{:S(2)}) copy-start(bf16[64,256]{1,0:T(8,128)(2,1)} %param.11) | copy-start | bytes 98308
  8.0 103.4 %all-gather.3.cloned.1.call-start = ((), (), s32[]{:S(2)}) async-start(), calls=%async_computation.1 | async-start | bytes 2162688 | tf_op jit(solution)/shard_map/all_gather | solution.py:40
  8.7 174.5 %all-reduce.2.cloned.1.call-start = ((), (), s32[]{:S(2)}) async-start(), calls=%async_computation.3 | async-start | bytes 229376 | tf_op jit(solution)/shard_map/psum | solution.py:37
  11.8 268.4 %copy-start.1 = (s32[448,256]{1,0:T(8,128)S(1)}, s32[448,256]{1,0:T(8,128)}, u32[]{:S(2)}) copy-start(s32[448,256]{1,0:T(8,128)} %param.17) | copy-start | bytes 1376260
  11.8 268.4 %copy-start.2 = (bf16[448,256]{1,0:T(8,128)(2,1)S(1)}, bf16[448,256]{1,0:T(8,128)(2,1)}, u32[]{:S(2)}) copy-start(bf16[448,256]{1,0:T(8,128)(2,1)} %param.15) | copy-start | bytes 688132
  11.8 268.3 %reduce-scatter.2.cloned.1.call-start = ((), (), s32[]{:S(2)}) async-start(), calls=%async_computation.2 | async-start | bytes 3899392 | tf_op jit(solution)/shard_map/reduce_scatter | solution.py:43
  116.0 165.6 %copy-start.3 = (bf16[448,256]{1,0:T(8,128)(2,1)S(1)}, bf16[448,256]{1,0:T(8,128)(2,1)}, u32[]{:S(2)}) copy-start(bf16[448,256]{1,0:T(8,128)(2,1)} %param.14) | copy-start | bytes 688132
  116.0 165.6 %copy-start.4 = (bf16[448,256]{1,0:T(8,128)(2,1)S(1)}, bf16[448,256]{1,0:T(8,128)(2,1)}, u32[]{:S(2)}) copy-start(bf16[448,256]{1,0:T(8,128)(2,1)} %param.16) | copy-start | bytes 688132
  116.0 259.4 %all-gather.5.cloned.1.call-start = ((), (), s32[]{:S(2)}) async-start(), calls=%async_computation.4 | async-start | bytes 3899392 | tf_op jit(solution)/shard_map/all_gather | solution.py:70
  281.6 3.1 copy-start.5
Sparse Core Ops, SparseCore 0:
  12.5 98.9 all-gather.2
Sparse Core Ops, SparseCore 1:
  12.7 170.5 all-reduce.1
  186.8 93.3 reduce-scatter.1
  284.8 90.5 all-gather.4
where the time goes:
time: 388 us; the launch traced here: 387 us
  waiting for transfers between devices  355 us (91%)
  between operations  15.7 us (4%)
  matrix products  9.97 us (3%)
  local copies, waits for them, and re-layouts  4.33 us (1%)
    all_gather x1, waiting for transfers between devices, on_device(): lax.all_gather(cot_mean, 'zero', axis=1, tiled=True)  99.6 us
    reduce_scatter x1, waiting for transfers between devices, on_device(): lax.psum_scatter(terms.astype(jnp.bfloat16), 'dp', scatter_dimension=1, t...  96.9 us
    all_gather x1, waiting for transfers between devices, on_device(): new_weight = lax.all_gather(weight_piece, 'dp', axis=1, tiled=True)  90.7 us
    psum x1, waiting for transfers between devices, on_device(): lax.psum(label_part.astype(jnp.bfloat16), 'dp').astype(jnp.float32)  67.2 us
  transfers between devices with their start and end apart: 4, of which 4 were waited for; matrix products, arithmetic and copies ran while one was open for 2% of the time, Pallas kernels for 0%

commit v1 on v0

v1 whole, which is shorter than its diff:
```python
import math

import jax
import jax.numpy as jnp
from jax import lax
from jax.experimental import pallas as pl
from jax.experimental.pallas import tpu as pltpu
from jax.sharding import PartitionSpec as P

beta_one = 0.965
beta_two = 0.99
gamma_rate = 0.5
learn_rate = 0.05
decay_rate = 0.1

NX, NL, NY, NH, NC = 4, 4, 8, 2, 2
NZ = NH * NL
ROWS, TOK, COLS, HALF, CAND = 448, 256, 256, 128, 64
PARTS = 4
STEP = ROWS // PARTS
TOP = ROWS // 2
BF16, F32, I32 = jnp.bfloat16, jnp.float32, jnp.int32


def device(x, y, zh, zl, core):
    return (zl * NX + x, (y * NH + zh) * NC + core)


def remote(src, dst, send, recv, to):
    return pltpu.make_async_remote_copy(
        src, dst, send, recv, device_id=to, device_id_type=pl.DeviceIdType.MESH
    )


def arrived(dst, sem):
    pltpu.make_async_copy(dst, dst, sem).wait()


def step_kernel(
    gate_in, cot_in, rows_in, true_in, sampled_in, weight_in, moment_in, curv_in, bits_in,
    wout, mout, cout,
    gate_v, cot_v, rows_v, true_v, sampled_v, weight_v, moment_v, curv_v, bits_v,
    hid, labs, cot, part, own_part, first, second, lab_sum, wide_rows, corr,
    load_sem, own_cot_send, cot_recv, chain_send, sib_send, sib_recv,
    hid_send, hid_recv, labs_send, labs_recv, sum_send, sum_recv,
    first_send, first_recv, second_send, second_recv, out_send, out_recv,
):
    dp = lax.axis_index("dp")
    zero = lax.axis_index("zero")
    x, zl = dp % NX, dp // NX
    core, zh, y = zero % NC, (zero // NC) % NH, zero // (NC * NH)
    z = zh * NL + zl
    xr, xo, xl = (x + 1) % NX, (x + 2) % NX, (x + 3) % NX
    right, across, left = [device(v, y, zh, zl, core) for v in (xr, xo, xl)]
    y_up, y_down = [device(x, (y + d) % NY, zh, zl, core) for d in (1, NY - 1)]
    sibling = device(x, y, zh, zl, 1 - core)
    line = [(zl + k) % NL for k in range(1, NL)]
    line_dev = [device(x, y, zh, v, core) for v in line]

    loads = [
        pltpu.make_async_copy(src, dst, load_sem.at[n])
        for n, (src, dst) in enumerate([
            (cot_in, cot_v), (gate_in, gate_v), (true_in, true_v), (sampled_in, sampled_v),
            (rows_in, rows_v), (moment_in, moment_v), (curv_in, curv_v), (bits_in, bits_v),
            (weight_in, weight_v),
        ])
    ]
    for load in loads:
        load.start()

    barrier = pltpu.get_barrier_semaphore()
    partners = [right, across, left, y_up, y_down, sibling]
    for k in range(1, NZ):
        other = (z + k) % NZ
        partners.append(device(x, y, other // NL, other % NL, core))
    for partner in partners:
        pl.semaphore_signal(
            barrier, inc=1, device_id=partner, device_id_type=pl.DeviceIdType.MESH
        )
    loads[0].wait()
    pl.semaphore_wait(barrier, len(partners))

    row = y // 2
    own_slot = cot.at[(y % 2) * 2 + zh, core, zl]

    def own_copy(h):
        return remote(
            cot_v, own_slot, own_cot_send.at[h], cot_recv.at[y % 2, z],
            device(x, y, h, row, core),
        )

    for h in range(NH):
        @pl.when(jnp.logical_or(zl != row, zh != h))
        def _():
            own_copy(h).start()

    @pl.when(zl == row)
    def _():
        pltpu.make_async_copy(cot_v, own_slot, cot_recv.at[y % 2, z]).start()

    loads[1].wait()
    gate = gate_v[0].astype(F32)
    up = gate_v[1].astype(F32)
    hid[zl] = (jax.nn.silu(gate) * up).astype(BF16)
    hid_copies = [
        remote(hid.at[zl], hid.at[zl], hid_send.at[k], hid_recv.at[zl], line_dev[k])
        for k in range(NL - 1)
    ]
    for copy in hid_copies:
        copy.start()
    loads[2].wait()
    loads[3].wait()
    labs[zl, 0:1] = true_v[...]
    labs[zl, 1:2] = sampled_v[...]
    labs[zl, 2:8] = jnp.zeros((6, TOK), I32)
    labs_copies = [
        remote(labs.at[zl], labs.at[zl], labs_send.at[k], labs_recv.at[zl], line_dev[k])
        for k in range(NL - 1)
    ]
    for copy in labs_copies:
        copy.start()

    place = (y - 2 * zl + NY) % NY
    lag = (
        jnp.where(place == 1, 1, (NY - place) % NY),
        jnp.where(place == 0, 1, place - 1),
    )
    goes_up = (place == 0, jnp.logical_and(place >= 1, place <= 6))
    goes_down = (jnp.logical_or(place == 0, place >= 3), place == 1)

    def slot_of(yb, k, half):
        return cot.at[yb * 2 + k // NL, half, k % NL]

    def chain_copies(yb, k):
        slot = slot_of(yb, k, core)
        return (
            remote(slot, slot, chain_send.at[yb, k, 0], cot_recv.at[yb, k], y_up),
            remote(slot, slot, chain_send.at[yb, k, 1], cot_recv.at[yb, k], y_down),
            remote(slot, slot, sib_send.at[yb, k], sib_recv.at[yb, k], sibling),
        )

    def chain_step(t, carry):
        for yb in (0, 1):
            k = t - lag[yb]

            @pl.when(jnp.logical_and(k >= 0, k < NZ))
            def _():
                arrived(slot_of(yb, k, core), cot_recv.at[yb, k])
                up_copy, down_copy, sib_copy = chain_copies(yb, k)

                @pl.when(goes_up[yb])
                def _():
                    up_copy.start()

                @pl.when(goes_down[yb])
                def _():
                    down_copy.start()

                sib_copy.start()

        return carry

    lax.fori_loop(0, NZ + 6, chain_step, 0)

    for v in line:
        arrived(hid.at[v], hid_recv.at[v])
        arrived(labs.at[v], labs_recv.at[v])
    classes = lax.broadcasted_iota(I32, (CAND, TOK), 0)
    total = jnp.zeros((ROWS, 2 * CAND), F32)
    for v in range(NL):
        lab = labs[v]
        hot = jnp.concatenate(
            [(classes == lab[n:n + 1]).astype(F32) for n in (0, 1)], axis=0
        ).astype(BF16)
        total += lax.dot_general(
            hid[v], hot, (((1,), (1,)), ((), ())), preferred_element_type=F32
        )
    lab_sum[x] = total.astype(BF16)
    sum_copies = [
        remote(lab_sum.at[x], lab_sum.at[x], sum_send.at[n], sum_recv.at[x], to)
        for n, to in enumerate((right, across, left))
    ]

    def wait_sibling(k, carry):
        for yb in (0, 1):
            arrived(slot_of(yb, k, 1 - core), sib_recv.at[yb, k])
        return carry

    lax.fori_loop(0, NZ, wait_sibling, 0)

    def partial_of(owner):
        acc = jnp.zeros((ROWS, COLS), F32)
        for v in range(NL):
            wide = jnp.concatenate([cot[owner, 0, v], cot[owner, 1, v]], axis=1)
            acc += jnp.dot(hid[v], wide, preferred_element_type=F32)
        return acc

    part[2] = partial_of(xo).astype(BF16)
    first_copies = [
        remote(part.at[2, pl.ds(0, TOP)], first.at[0], first_send.at[0], first_recv.at[0], right),
        remote(part.at[2, pl.ds(TOP, TOP)], first.at[1], first_send.at[1], first_recv.at[1], left),
    ]
    for copy in first_copies:
        copy.start()
    for copy in sum_copies:
        copy.start()
    part[1] = partial_of(xr).astype(BF16)
    part[3] = partial_of(xl).astype(BF16)

    def second_copies(q):
        rows = pl.ds(q * STEP, STEP)
        return (
            remote(part.at[1, rows], second.at[0, rows], second_send.at[0, q],
                   second_recv.at[0, q], right),
            remote(part.at[3, rows], second.at[1, rows], second_send.at[1, q],
                   second_recv.at[1, q], left),
        )

    half = PARTS // 2
    for q in range(half):
        second_copies(half + q)[0].start()
        second_copies(q)[1].start()
    arrived(first.at[0], first_recv.at[0])
    arrived(first.at[1], first_recv.at[1])
    for q in range(half):
        rows = pl.ds(q * STEP, STEP)
        low = pl.ds(TOP + q * STEP, STEP)
        part[1, rows] = (part[1, rows].astype(F32) + first[0, rows].astype(F32)).astype(BF16)
        second_copies(q)[0].start()
        part[3, low] = (part[3, low].astype(F32) + first[1, rows].astype(F32)).astype(BF16)
        second_copies(half + q)[1].start()
    own_part[...] = partial_of(x)

    loads[4].wait()
    blank = jnp.zeros((CAND, COLS), BF16)
    wide_rows[0:CAND, 0:COLS] = rows_v[...]
    wide_rows[0:CAND, COLS:2 * COLS] = blank
    wide_rows[CAND:2 * CAND, 0:COLS] = blank
    wide_rows[CAND:2 * CAND, COLS:2 * COLS] = rows_v[...]
    for v in (xl, xr, xo):
        arrived(lab_sum.at[v], sum_recv.at[v])
    rest = jnp.zeros((ROWS, 2 * CAND), F32)
    for v in range(NX):
        rest += lab_sum[v].astype(F32)
    terms = []
    for _ in range(3):
        term = rest.astype(BF16)
        terms.append(term)
        rest = rest - term.astype(F32)
    spread = wide_rows[...]
    corr[...] = (
        jnp.dot(terms[2], spread, preferred_element_type=F32)
        + jnp.dot(terms[1], spread, preferred_element_type=F32)
    ) + jnp.dot(terms[0], spread, preferred_element_type=F32)

    for n in (5, 6, 7, 8):
        loads[n].wait()
    factor = 1.0 / math.sqrt(TOK * NX * NL)

    def out_copy(q, index, n, to):
        piece = wout.at[index, pl.ds(q * STEP, STEP)]
        return remote(piece, piece, out_send.at[q, n], out_recv.at[q, index], to)

    def own_sends(q):
        return [out_copy(q, dp, n, to) for n, to in enumerate(line_dev + [right, left])]

    def line_sends(q):
        return [
            out_copy(q, v * NX + x, 5 + 2 * m + d, to)
            for m, v in enumerate(line) for d, to in enumerate((right, left))
        ]

    def forwards(q):
        order = [zl] + line
        return [
            out_copy(q, v * NX + (xl if m < 2 else xr), 11 + m, right if m < 2 else left)
            for m, v in enumerate(order)
        ]

    def out_arrived(q, index):
        arrived(wout.at[index, pl.ds(q * STEP, STEP)], out_recv.at[q, index])

    def finish(q, carry):
        rows = pl.ds(pl.multiple_of(q * STEP, STEP), STEP)
        arrived(second.at[0, rows], second_recv.at[0, q])
        arrived(second.at[1, rows], second_recv.at[1, q])
        common = (
            own_part[rows, :] + second[0, rows, :].astype(F32) + second[1, rows, :].astype(F32)
        )
        grad_true = (common - corr[rows, 0:COLS]) * factor
        grad_sampled = (common - corr[rows, COLS:2 * COLS]) * factor
        drawn = bits_v[rows, :]
        low = jnp.bitwise_and(drawn, 127)
        high = jnp.right_shift(drawn, 7)
        mixed = jnp.bitwise_and(3 * low + 5 * high, 127)

        def dither(value, noise):
            scale = (noise.astype(F32) + 960.5) * (1.0 / 1024.0)
            return (value * scale).astype(BF16)

        new_moment = dither(
            beta_one * moment_v[rows, :].astype(F32) + (1.0 - beta_one) * grad_true, low
        )
        new_curv = dither(
            beta_two * curv_v[rows, :].astype(F32)
            + (1.0 - beta_two) * grad_sampled * grad_sampled,
            high,
        )
        ratio = jnp.clip(
            new_moment.astype(F32) / (gamma_rate * new_curv.astype(F32)), -1.0, 1.0
        )
        shrunk = (
            weight_v[rows, :].astype(F32) * (1.0 - learn_rate * decay_rate) - learn_rate * ratio
        )
        mout[rows, :] = new_moment
        cout[rows, :] = new_curv
        wout[dp, rows, :] = dither(shrunk, mixed)
        for copy in own_sends(q):
            copy.start()
        return carry

    lax.fori_loop(0, PARTS, finish, 0)

    def pass_line(q):
        for m, v in enumerate(line):
            out_arrived(q, v * NX + x)
            line_sends(q)[2 * m].start()
            line_sends(q)[2 * m + 1].start()

    def pass_ring(q):
        copies = forwards(q)
        for m, v in enumerate([zl] + line):
            out_arrived(q, v * NX + xl)
            out_arrived(q, v * NX + xr)
            copies[m].start()

    def spread_step(t, carry):
        @pl.when(t < PARTS)
        def _():
            pass_line(t)

        @pl.when(t > 0)
        def _():
            pass_ring(t - 1)

        return carry

    lax.fori_loop(0, PARTS + 1, spread_step, 0)

    def last_step(q, carry):
        for v in [zl] + line:
            out_arrived(q, v * NX + xo)
        for copy in own_sends(q) + line_sends(q) + forwards(q):
            copy.wait_send()
        for copy in second_copies(q):
            copy.wait_send()
        return carry

    lax.fori_loop(0, PARTS, last_step, 0)

    for h in range(NH):
        @pl.when(jnp.logical_or(zl != row, zh != h))
        def _():
            own_copy(h).wait_send()

    for copy in hid_copies + labs_copies + sum_copies + first_copies:
        copy.wait_send()

    def drain_chain(k, carry):
        for yb in (0, 1):
            up_copy, down_copy, sib_copy = chain_copies(yb, k)

            @pl.when(goes_up[yb])
            def _():
                up_copy.wait_send()

            @pl.when(goes_down[yb])
            def _():
                down_copy.wait_send()

            sib_copy.wait_send()

        return carry

    lax.fori_loop(0, NZ, drain_chain, 0)


def place_kernel(wide, moment, curv, wide_out, moment_out, curv_out, sem):
    copies = [
        pltpu.make_async_copy(
            wide.at[n], wide_out.at[:, pl.ds(n * COLS, COLS)], sem.at[n]
        )
        for n in range(NX * NL)
    ]
    copies.append(pltpu.make_async_copy(moment, moment_out, sem.at[NX * NL]))
    copies.append(pltpu.make_async_copy(curv, curv_out, sem.at[NX * NL + 1]))
    for copy in copies:
        copy.start()
    for copy in copies:
        copy.wait()


def on_device(
    gate_up, cot_mean, label_rows, true_labels, sampled_labels, weight, moment, curvature, bits
):
    dma = pltpu.SemaphoreType.DMA
    groups = NX * NL
    anywhere = pl.BlockSpec(memory_space=pl.ANY)
    in_vmem = pl.BlockSpec(memory_space=pltpu.VMEM)
    state = (ROWS, COLS)
    pieces, new_moment, new_curv = pl.pallas_call(
        step_kernel,
        out_shape=[
            pltpu.VMEM((groups, ROWS, COLS), BF16),
            pltpu.VMEM(state, BF16),
            pltpu.VMEM(state, BF16),
        ],
        in_specs=[anywhere] * 9,
        out_specs=[in_vmem] * 3,
        scratch_shapes=[
            pltpu.VMEM((2, ROWS, TOK), BF16),
            pltpu.VMEM((TOK, HALF), BF16),
            pltpu.VMEM((CAND, COLS), BF16),
            pltpu.VMEM((1, TOK), I32),
            pltpu.VMEM((1, TOK), I32),
            pltpu.VMEM(state, BF16),
            pltpu.VMEM(state, BF16),
            pltpu.VMEM(state, BF16),
            pltpu.VMEM(state, I32),
            pltpu.VMEM((NL, ROWS, TOK), BF16),
            pltpu.VMEM((NL, 8, TOK), I32),
            pltpu.VMEM((NX, NC, NL, TOK, HALF), BF16),
            pltpu.VMEM((NX, ROWS, COLS), BF16),
            pltpu.VMEM(state, F32),
            pltpu.VMEM((2, TOP, COLS), BF16),
            pltpu.VMEM((2, ROWS, COLS), BF16),
            pltpu.VMEM((NX, ROWS, 2 * CAND), BF16),
            pltpu.VMEM((2 * CAND, 2 * COLS), BF16),
            pltpu.VMEM((ROWS, 2 * COLS), F32),
            dma((9,)),
            dma((NH,)),
            dma((2, NZ)),
            dma((2, NZ, 2)),
            dma((2, NZ)),
            dma((2, NZ)),
            dma((NL - 1,)),
            dma((NL,)),
            dma((NL - 1,)),
            dma((NL,)),
            dma((3,)),
            dma((NX,)),
            dma((2,)),
            dma((2,)),
            dma((2, PARTS)),
            dma((2, PARTS)),
            dma((PARTS, 15)),
            dma((PARTS, groups)),
        ],
        compiler_params=pltpu.CompilerParams(
            collective_id=0, has_side_effects=True, vmem_limit_bytes=32 * 1024 * 1024
        ),
        cost_estimate=pl.CostEstimate(
            flops=1_000_000_000, bytes_accessed=6_000_000, transcendentals=114_688
        ),
        name="sophia_step",
    )(
        jnp.swapaxes(gate_up, 1, 2), cot_mean, label_rows,
        true_labels.reshape(1, TOK), sampled_labels.reshape(1, TOK),
        weight, moment, curvature, bits,
    )
    return pl.pallas_call(
        place_kernel,
        out_shape=[
            jax.ShapeDtypeStruct((ROWS, groups * COLS), BF16),
            jax.ShapeDtypeStruct(state, BF16),
            jax.ShapeDtypeStruct(state, BF16),
        ],
        in_specs=[in_vmem] * 3,
        out_specs=[anywhere] * 3,
        scratch_shapes=[dma((groups + 2,))],
        name="place",
    )(pieces, new_moment, new_curv)


def solution(mesh):
    in_specs = (
        P(None, "dp", "zero"),
        P("dp", "zero"),
        P(None, "dp"),
        P("dp"),
        P("dp"),
        P("zero", "dp"),
        P("zero", "dp"),
        P("zero", "dp"),
        P("zero", "dp"),
    )
    out_specs = (P("zero", None), P("zero", "dp"), P("zero", "dp"))
    return jax.shard_map(
        on_device, mesh=mesh, in_specs=in_specs, out_specs=out_specs, check_vma=False
    )
```

time: 388 us -> 134 us (0.35)
  the two profiles are of different devices: /device:TPU:4 before, /device:TPU:8 now
where the time goes in v1:
time: 134 us; the launch traced here: 133 us
  Pallas kernels  122 us (91%)
  local copies, waits for them, and re-layouts  11 us (8%)
    pallas_call x1, Pallas kernels, on_device(): pl.pallas_call(step_kernel, out_shape=[pltpu.VMEM((groups, ROWS, COLS), B...  117 us
    unnamed x24, local copies, waits for them, and re-layouts  11 us
    pallas_call x1, Pallas kernels, on_device(): pl.pallas_call(place_kernel, out_shape=[jax.ShapeDtypeStruct((ROWS, group...  4.3 us

profile of v1, /device:TPU:8, one launch (start us, length us, event | category | flops | bytes accessed | tf_op | source)
XLA Modules:
  0.0 133.4 jit_solution(4544979977931111746)
XLA Ops:
  0.6 0.0 copy-start.3
  0.6 1.0 copy-done.3
  1.7 0.0 copy-start.4
  1.7 1.0 copy-done.4
  2.7 0.0 copy-start.5
  2.7 0.9 copy-done.5
  3.6 0.0 copy-start.6
  3.6 0.9 copy-done.6
  4.5 0.0 copy-start.7
  4.6 0.9 copy-done.7
  5.5 0.0 copy-start.8
  5.5 0.8 copy-done.8
  6.3 0.0 copy-start.9
  6.3 0.8 copy-done.9
  7.1 0.0 copy-start.10
  7.1 0.7 copy-done.10
  7.8 0.0 copy-start.11
  7.8 0.7 copy-done.11
  8.4 117.5 %sophia_step.1 = (bf16[16,448,256]{2,1,0:T(8,128)(2,1)S(1)}, bf16[448,256]{1,0:T(8,128)(2,1)S(1)}, bf16[448,256]{1,0:T(8,128)(2,1)S(1)}) custom-call(bf16[2,448,256]{2,1,0:T(8,128)(2,1)S(1)} %bitcast.3, bf16[256,128]{1,0:T(8,128)(2,1)S(1)} %copy-done.8, bf16[64,256]{1,0:T(8,128)(2,1)S(1)} %copy-done.9, s32[1,256]{1,0:T(1,128)S(1)} %bitcast.4, ...), custom_call_target="tpu_custom_call" | custom-call | flops 1000000000 | bytes 6000000 | tf_op jit(solution)/shard_map/sophia_step/pallas_call | solution.py:411
  125.9 0.0 copy-start
  125.9 1.8 %copy-done = bf16[16,448,256]{2,1,0:T(8,128)(2,1)} copy-done((bf16[16,448,256]{2,1,0:T(8,128)(2,1)}, bf16[16,448,256]{2,1,0:T(8,128)(2,1)S(1)}, u32[]{:S(2)}) %copy-start) | copy-done | bytes 3670040
  127.7 0.7 copy-done.1
  128.4 0.7 copy-done.2
  129.1 4.3 %place.1 = (bf16[448,4096]{1,0:T(8,128)(2,1)}, bf16[448,256]{1,0:T(8,128)(2,1)}, bf16[448,256]{1,0:T(8,128)(2,1)}) custom-call(bf16[16,448,256]{2,1,0:T(8,128)(2,1)} %copy-done, bf16[448,256]{1,0:T(8,128)(2,1)} %copy-done.1, bf16[448,256]{1,0:T(8,128)(2,1)} %copy-done.2), custom_call_target="tpu_custom_call" | custom-call | tf_op jit(solution)/shard_map/place/pallas_call | solution.py:471
  (2 shorter events, 0.0 us)
Async XLA Ops:
  0.6 1.0 copy-start.3
  1.7 1.0 copy-start.4
  2.7 0.9 copy-start.5
  3.6 0.9 copy-start.6
  4.5 0.9 copy-start.7
  5.5 0.8 copy-start.8
  6.3 0.8 copy-start.9
  7.1 0.7 copy-start.10
  7.8 0.7 copy-start.11
  125.9 1.8 %copy-start = (bf16[16,448,256]{2,1,0:T(8,128)(2,1)}, bf16[16,448,256]{2,1,0:T(8,128)(2,1)S(1)}, u32[]{:S(2)}) copy-start(bf16[16,448,256]{2,1,0:T(8,128)(2,1)S(1)} %get-tuple-element.6.wide) | copy-start | bytes 11010052
  127.7 0.7 copy-start.1
  128.4 0.7 copy-start.2

commit v2 on v1

--- a/solution.py
+++ b/solution.py
@@ -17,6 +17,9 @@
 NZ = NH * NL
 ROWS, TOK, COLS, HALF, CAND = 448, 256, 256, 128, 64
 PARTS = 4
+SUB, LAG = 1, 3
+BLOCKS = NZ * SUB
+FINE = TOK // SUB
 STEP = ROWS // PARTS
 TOP = ROWS // 2
 BF16, F32, I32 = jnp.bfloat16, jnp.float32, jnp.int32
@@ -70,9 +73,12 @@
 
     barrier = pltpu.get_barrier_semaphore()
     partners = [right, across, left, y_up, y_down, sibling]
-    for k in range(1, NZ):
+    y_far = (y + NY // 2) % NY
+    for k in range(NZ):
         other = (z + k) % NZ
-        partners.append(device(x, y, other // NL, other % NL, core))
+        if k:
+            partners.append(device(x, y, other // NL, other % NL, core))
+        partners.append(device(x, y_far, other // NL, other % NL, core))
     for partner in partners:
         pl.semaphore_signal(
             barrier, inc=1, device_id=partner, device_id_type=pl.DeviceIdType.MESH
@@ -83,20 +89,30 @@
     row = y // 2
     own_slot = cot.at[(y % 2) * 2 + zh, core, zl]
 
-    def own_copy(h):
+    def fine_of(ref, n):
+        return ref.at[pl.ds(n * FINE, FINE)]
+
+    def own_copy(far, h, n):
         return remote(
-            cot_v, own_slot, own_cot_send.at[h], cot_recv.at[y % 2, z],
-            device(x, y, h, row, core),
+            fine_of(cot_v, n), fine_of(own_slot, n), own_cot_send.at[far, h, n],
+            cot_recv.at[y % 2, z, n], device(x, (y, y_far)[far], h, row, core),
         )
 
     for h in range(NH):
         @pl.when(jnp.logical_or(zl != row, zh != h))
         def _():
-            own_copy(h).start()
+            for n in range(SUB):
+                own_copy(0, h, n).start()
+
+        for n in range(SUB):
+            own_copy(1, h, n).start()
 
     @pl.when(zl == row)
     def _():
-        pltpu.make_async_copy(cot_v, own_slot, cot_recv.at[y % 2, z]).start()
+        for n in range(SUB):
+            pltpu.make_async_copy(
+                fine_of(cot_v, n), fine_of(own_slot, n), cot_recv.at[y % 2, z, n]
+            ).start()
 
     loads[1].wait()
     gate = gate_v[0].astype(F32)
@@ -120,32 +136,35 @@
     for copy in labs_copies:
         copy.start()
 
-    place = (y - 2 * zl + NY) % NY
+    place = (y - 2 * zl + NY) % (NY // 2)
     lag = (
-        jnp.where(place == 1, 1, (NY - place) % NY),
+        jnp.where(place == 1, 1, (4 - place) % 4),
         jnp.where(place == 0, 1, place - 1),
     )
-    goes_up = (place == 0, jnp.logical_and(place >= 1, place <= 6))
-    goes_down = (jnp.logical_or(place == 0, place >= 3), place == 1)
+    goes_up = (place == 0, jnp.logical_or(place == 1, place == 2))
+    goes_down = (jnp.logical_or(place == 0, place == 3), place == 1)
 
     def slot_of(yb, k, half):
-        return cot.at[yb * 2 + k // NL, half, k % NL]
+        step, n = k // SUB, k % SUB
+        src = jnp.where(step % 2 == 1, z + (step + 1) // 2, z + NZ - step // 2) % NZ
+        return cot.at[yb * 2 + src // NL, half, src % NL, pl.ds(n * FINE, FINE)], src, n
 
     def chain_copies(yb, k):
-        slot = slot_of(yb, k, core)
+        slot, src, n = slot_of(yb, k, core)
         return (
-            remote(slot, slot, chain_send.at[yb, k, 0], cot_recv.at[yb, k], y_up),
-            remote(slot, slot, chain_send.at[yb, k, 1], cot_recv.at[yb, k], y_down),
+            remote(slot, slot, chain_send.at[yb, k, 0], cot_recv.at[yb, src, n], y_up),
+            remote(slot, slot, chain_send.at[yb, k, 1], cot_recv.at[yb, src, n], y_down),
             remote(slot, slot, sib_send.at[yb, k], sib_recv.at[yb, k], sibling),
         )
 
     def chain_step(t, carry):
         for yb in (0, 1):
-            k = t - lag[yb]
-
-            @pl.when(jnp.logical_and(k >= 0, k < NZ))
+            k = t - LAG * lag[yb]
+
+            @pl.when(jnp.logical_and(k >= 0, k < BLOCKS))
             def _():
-                arrived(slot_of(yb, k, core), cot_recv.at[yb, k])
+                slot, src, n = slot_of(yb, k, core)
+                arrived(slot, cot_recv.at[yb, src, n])
                 up_copy, down_copy, sib_copy = chain_copies(yb, k)
 
                 @pl.when(goes_up[yb])
@@ -160,7 +179,7 @@
 
         return carry
 
-    lax.fori_loop(0, NZ + 6, chain_step, 0)
+    lax.fori_loop(0, BLOCKS + 2 * LAG, chain_step, 0)
 
     for v in line:
         arrived(hid.at[v], hid_recv.at[v])
@@ -183,10 +202,10 @@
 
     def wait_sibling(k, carry):
         for yb in (0, 1):
-            arrived(slot_of(yb, k, 1 - core), sib_recv.at[yb, k])
+            arrived(slot_of(yb, k, 1 - core)[0], sib_recv.at[yb, k])
         return carry
 
-    lax.fori_loop(0, NZ, wait_sibling, 0)
+    lax.fori_loop(0, BLOCKS, wait_sibling, 0)
 
     def partial_of(owner):
         acc = jnp.zeros((ROWS, COLS), F32)
@@ -361,9 +380,16 @@
     for h in range(NH):
         @pl.when(jnp.logical_or(zl != row, zh != h))
         def _():
-            own_copy(h).wait_send()
-
-    for copy in hid_copies + labs_copies + sum_copies + first_copies:
+            for n in range(SUB):
+                own_copy(0, h, n).wait_send()
+
+        for n in range(SUB):
+            own_copy(1, h, n).wait_send()
+    for copy in hid_copies + labs_copies:
+        copy.wait_send()
+    for copy in sum_copies:
+        copy.wait_send()
+    for copy in first_copies:
         copy.wait_send()
 
     def drain_chain(k, carry):
@@ -382,7 +408,7 @@
 
         return carry
 
-    lax.fori_loop(0, NZ, drain_chain, 0)
+    lax.fori_loop(0, BLOCKS, drain_chain, 0)
 
 
 def place_kernel(wide, moment, curv, wide_out, moment_out, curv_out, sem):
@@ -406,6 +432,7 @@
     dma = pltpu.SemaphoreType.DMA
     groups = NX * NL
     anywhere = pl.BlockSpec(memory_space=pl.ANY)
+    in_hbm = pl.BlockSpec(memory_space=pltpu.HBM)
     in_vmem = pl.BlockSpec(memory_space=pltpu.VMEM)
     state = (ROWS, COLS)
     pieces, new_moment, new_curv = pl.pallas_call(
@@ -415,7 +442,7 @@
             pltpu.VMEM(state, BF16),
             pltpu.VMEM(state, BF16),
         ],
-        in_specs=[anywhere] * 9,
+        in_specs=[in_hbm] * 9,
         out_specs=[in_vmem] * 3,
         scratch_shapes=[
             pltpu.VMEM((2, ROWS, TOK), BF16),
@@ -438,11 +465,11 @@
             pltpu.VMEM((2 * CAND, 2 * COLS), BF16),
             pltpu.VMEM((ROWS, 2 * COLS), F32),
             dma((9,)),
-            dma((NH,)),
-            dma((2, NZ)),
-            dma((2, NZ, 2)),
-            dma((2, NZ)),
-            dma((2, NZ)),
+            dma((2, NH, SUB)),
+            dma((2, NZ, SUB)),
+            dma((2, BLOCKS, 2)),
+            dma((2, BLOCKS)),
+            dma((2, BLOCKS)),
             dma((NL - 1,)),
             dma((NL,)),
             dma((NL - 1,)),
@@ -457,7 +484,7 @@
             dma((PARTS, groups)),
         ],
         compiler_params=pltpu.CompilerParams(
-            collective_id=0, has_side_effects=True, vmem_limit_bytes=32 * 1024 * 1024
+            collective_id=0, has_side_effects=True, vmem_limit_bytes=58 * 1024 * 1024
         ),
         cost_estimate=pl.CostEstimate(
             flops=1_000_000_000, bytes_accessed=6_000_000, transcendentals=114_688
@@ -475,9 +502,10 @@
             jax.ShapeDtypeStruct(state, BF16),
             jax.ShapeDtypeStruct(state, BF16),
         ],
-        in_specs=[in_vmem] * 3,
-        out_specs=[anywhere] * 3,
+        in_specs=[anywhere] * 3,
+        out_specs=[in_hbm] * 3,
         scratch_shapes=[dma((groups + 2,))],
+        compiler_params=pltpu.CompilerParams(vmem_limit_bytes=1024 * 1024),
         name="place",
     )(pieces, new_moment, new_curv)
 

time: 134 us -> 101 us (0.75)
  the two profiles are of different devices: /device:TPU:8 before, /device:TPU:64 now
where the time goes in v2:
time: 101 us
  Pallas kernels  101 us (100%)
    pallas_call x1, Pallas kernels, on_device(): pl.pallas_call(step_kernel, out_shape=[pltpu.VMEM((groups, ROWS, COLS), B...  98.5 us
    pallas_call x1, Pallas kernels, on_device(): pl.pallas_call(place_kernel, out_shape=[jax.ShapeDtypeStruct((ROWS, group...  2.13 us

profile of v2, /device:TPU:64, one launch (start us, length us, event | category | flops | bytes accessed | tf_op | source)
XLA Modules:
  0.0 101.3 jit_solution(8958543279281923450)
XLA Ops:
  0.6 98.5 %sophia_step.1 = (bf16[16,448,256]{2,1,0:T(8,128)(2,1)S(1)}, bf16[448,256]{1,0:T(8,128)(2,1)S(1)}, bf16[448,256]{1,0:T(8,128)(2,1)S(1)}) custom-call(bf16[2,448,256]{2,1,0:T(8,128)(2,1)} %bitcast.3, bf16[256,128]{1,0:T(8,128)(2,1)} %cot_in.1, bf16[64,256]{1,0:T(8,128)(2,1)} %rows_in.1, s32[1,256]{1,0:T(1,128)} %bitcast.4, s32[1,256]{1,0:T(1,128)} %bitcast.5, ...), custom_call_target="tpu_custom_call" | custom-call | flops 1000000000 | bytes 6000000 | tf_op jit(solution)/shard_map/sophia_step/pallas_call | solution.py:438
  99.2 2.1 %place.1 = (bf16[448,4096]{1,0:T(8,128)(2,1)}, bf16[448,256]{1,0:T(8,128)(2,1)}, bf16[448,256]{1,0:T(8,128)(2,1)}) custom-call(bf16[16,448,256]{2,1,0:T(8,128)(2,1)S(1)} %get-tuple-element.6.wide, bf16[448,256]{1,0:T(8,128)(2,1)S(1)} %get-tuple-element.7.moment, bf16[448,256]{1,0:T(8,128)(2,1)S(1)} %get-tuple-element.8.curv), custom_call_target="tpu_custom_call" | custom-call | tf_op jit(solution)/shard_map/place/pallas_call | solution.py:498

commit v3 on v2

--- a/solution.py
+++ b/solution.py
@@ -18,6 +18,7 @@
 ROWS, TOK, COLS, HALF, CAND = 448, 256, 256, 128, 64
 PARTS = 4
 SUB, LAG = 1, 3
+HID_AT, CUT_AT = 4, 11
 BLOCKS = NZ * SUB
 FINE = TOK // SUB
 STEP = ROWS // PARTS
@@ -43,9 +44,10 @@
     gate_in, cot_in, rows_in, true_in, sampled_in, weight_in, moment_in, curv_in, bits_in,
     wout, mout, cout,
     gate_v, cot_v, rows_v, true_v, sampled_v, weight_v, moment_v, curv_v, bits_v,
-    hid, labs, cot, part, own_part, first, second, lab_sum, wide_rows, corr,
+    hid, cot, part, own_part, first, second, lab_own, lab_cut, lab_sum, lab_all,
+    wide_rows, corr,
     load_sem, own_cot_send, cot_recv, chain_send, sib_send, sib_recv,
-    hid_send, hid_recv, labs_send, labs_recv, sum_send, sum_recv,
+    hid_send, hid_recv, cut_send, cut_recv, sum_send, sum_recv, all_send, all_recv,
     first_send, first_recv, second_send, second_recv, out_send, out_recv,
 ):
     dp = lax.axis_index("dp")
@@ -57,7 +59,7 @@
     right, across, left = [device(v, y, zh, zl, core) for v in (xr, xo, xl)]
     y_up, y_down = [device(x, (y + d) % NY, zh, zl, core) for d in (1, NY - 1)]
     sibling = device(x, y, zh, zl, 1 - core)
-    line = [(zl + k) % NL for k in range(1, NL)]
+    line = [zl + 1 - 2 * (zl % 2), (zl + 2) % NL, NL - 1 - zl]
     line_dev = [device(x, y, zh, v, core) for v in line]
 
     loads = [
@@ -72,47 +74,29 @@
         load.start()
 
     barrier = pltpu.get_barrier_semaphore()
-    partners = [right, across, left, y_up, y_down, sibling]
     y_far = (y + NY // 2) % NY
-    for k in range(NZ):
-        other = (z + k) % NZ
-        if k:
-            partners.append(device(x, y, other // NL, other % NL, core))
-        partners.append(device(x, y_far, other // NL, other % NL, core))
-    for partner in partners:
+    row = y // 2
+
+    def greet(partner):
         pl.semaphore_signal(
             barrier, inc=1, device_id=partner, device_id_type=pl.DeviceIdType.MESH
         )
-    loads[0].wait()
-    pl.semaphore_wait(barrier, len(partners))
-
-    row = y // 2
-    own_slot = cot.at[(y % 2) * 2 + zh, core, zl]
-
-    def fine_of(ref, n):
-        return ref.at[pl.ds(n * FINE, FINE)]
-
-    def own_copy(far, h, n):
-        return remote(
-            fine_of(cot_v, n), fine_of(own_slot, n), own_cot_send.at[far, h, n],
-            cot_recv.at[y % 2, z, n], device(x, (y, y_far)[far], h, row, core),
-        )
-
-    for h in range(NH):
-        @pl.when(jnp.logical_or(zl != row, zh != h))
+
+    for y_from, at_row in ((y_far, zl == y_far // 2), (y, zl == row)):
+        @pl.when(at_row)
         def _():
-            for n in range(SUB):
-                own_copy(0, h, n).start()
-
-        for n in range(SUB):
-            own_copy(1, h, n).start()
-
-    @pl.when(zl == row)
+            for k in (4, 3, 5, 2, 6, 1, 7):
+                other = (z + k) % NZ
+                greet(device(x, y_from, other // NL, other % NL, core))
+
+    @pl.when(zl == y_far // 2)
     def _():
-        for n in range(SUB):
-            pltpu.make_async_copy(
-                fine_of(cot_v, n), fine_of(own_slot, n), cot_recv.at[y % 2, z, n]
-            ).start()
+        greet(device(x, y_far, zh, zl, core))
+
+    partners = [right, across, left, y_up, y_down, sibling] + line_dev
+    for partner in partners:
+        greet(partner)
+    greeted = len(partners) + 2 * NH - (zl == row).astype(I32)
 
     loads[1].wait()
     gate = gate_v[0].astype(F32)
@@ -122,18 +106,63 @@
         remote(hid.at[zl], hid.at[zl], hid_send.at[k], hid_recv.at[zl], line_dev[k])
         for k in range(NL - 1)
     ]
-    for copy in hid_copies:
-        copy.start()
     loads[2].wait()
     loads[3].wait()
-    labs[zl, 0:1] = true_v[...]
-    labs[zl, 1:2] = sampled_v[...]
-    labs[zl, 2:8] = jnp.zeros((6, TOK), I32)
-    labs_copies = [
-        remote(labs.at[zl], labs.at[zl], labs_send.at[k], labs_recv.at[zl], line_dev[k])
-        for k in range(NL - 1)
-    ]
-    for copy in labs_copies:
+    classes = lax.broadcasted_iota(I32, (CAND, TOK), 0)
+    hot = jnp.concatenate(
+        [(classes == lab[...]).astype(F32) for lab in (true_v, sampled_v)], axis=0
+    ).astype(BF16)
+    label_part = lax.dot_general(
+        hid[zl], hot, (((1,), (1,)), ((), ())), preferred_element_type=F32
+    )
+    for v in range(NL):
+        lab_own[v] = label_part[v * STEP:(v + 1) * STEP].astype(BF16)
+    cut_copies = [
+        remote(lab_own.at[v], lab_cut.at[zl], cut_send.at[k], cut_recv.at[zl], line_dev[k])
+        for k, v in enumerate(line)
+    ]
+    lab_cut[zl] = lab_own[zl]
+    ring = [xr, xo, xl]
+    sum_copies = [
+        remote(lab_sum.at[x], lab_sum.at[x], sum_send.at[k], sum_recv.at[x], to)
+        for k, to in enumerate((right, across, left))
+    ]
+    all_copies = [
+        remote(lab_all.at[zl], lab_all.at[zl], all_send.at[k], all_recv.at[zl], to)
+        for k, to in enumerate(line_dev)
+    ]
+
+    loads[0].wait()
+    pl.semaphore_wait(barrier, greeted)
+
+    own_slot = cot.at[(y % 2) * 2 + zh, core, zl]
+
+    def fine_of(ref, n):
+        return ref.at[pl.ds(n * FINE, FINE)]
+
+    def own_copy(far, h, n):
+        return remote(
+            fine_of(cot_v, n), fine_of(own_slot, n), own_cot_send.at[far, h, n],
+            cot_recv.at[y % 2, z, n], device(x, (y, y_far)[far], h, row, core),
+        )
+
+    for h in range(NH):
+        @pl.when(jnp.logical_or(zl != row, zh != h))
+        def _():
+            for n in range(SUB):
+                own_copy(0, h, n).start()
+
+        for n in range(SUB):
+            own_copy(1, h, n).start()
+
+    @pl.when(zl == row)
+    def _():
+        for n in range(SUB):
+            pltpu.make_async_copy(
+                fine_of(cot_v, n), fine_of(own_slot, n), cot_recv.at[y % 2, z, n]
+            ).start()
+
+    for copy in cut_copies:
         copy.start()
 
     place = (y - 2 * zl + NY) % (NY // 2)
@@ -179,26 +208,22 @@
 
         return carry
 
-    lax.fori_loop(0, BLOCKS + 2 * LAG, chain_step, 0)
+    lax.fori_loop(0, HID_AT, chain_step, 0)
+    for copy in hid_copies:
+        copy.start()
+    lax.fori_loop(HID_AT, CUT_AT, chain_step, 0)
+    for v in line:
+        arrived(lab_cut.at[v], cut_recv.at[v])
+    quarter = lab_cut[0].astype(F32)
+    for v in range(1, NL):
+        quarter += lab_cut[v].astype(F32)
+    lab_sum[x] = quarter
+    for copy in sum_copies:
+        copy.start()
+    lax.fori_loop(CUT_AT, BLOCKS + 2 * LAG, chain_step, 0)
 
     for v in line:
         arrived(hid.at[v], hid_recv.at[v])
-        arrived(labs.at[v], labs_recv.at[v])
-    classes = lax.broadcasted_iota(I32, (CAND, TOK), 0)
-    total = jnp.zeros((ROWS, 2 * CAND), F32)
-    for v in range(NL):
-        lab = labs[v]
-        hot = jnp.concatenate(
-            [(classes == lab[n:n + 1]).astype(F32) for n in (0, 1)], axis=0
-        ).astype(BF16)
-        total += lax.dot_general(
-            hid[v], hot, (((1,), (1,)), ((), ())), preferred_element_type=F32
-        )
-    lab_sum[x] = total.astype(BF16)
-    sum_copies = [
-        remote(lab_sum.at[x], lab_sum.at[x], sum_send.at[n], sum_recv.at[x], to)
-        for n, to in enumerate((right, across, left))
-    ]
 
     def wait_sibling(k, carry):
         for yb in (0, 1):
@@ -220,8 +245,6 @@
         remote(part.at[2, pl.ds(TOP, TOP)], first.at[1], first_send.at[1], first_recv.at[1], left),
     ]
     for copy in first_copies:
-        copy.start()
-    for copy in sum_copies:
         copy.start()
     part[1] = partial_of(xr).astype(BF16)
     part[3] = partial_of(xl).astype(BF16)
@@ -239,6 +262,11 @@
     for q in range(half):
         second_copies(half + q)[0].start()
         second_copies(q)[1].start()
+    for v in ring:
+        arrived(lab_sum.at[v], sum_recv.at[v])
+    lab_all[zl] = (lab_sum[0] + lab_sum[1]) + (lab_sum[2] + lab_sum[3])
+    for copy in all_copies:
+        copy.start()
     arrived(first.at[0], first_recv.at[0])
     arrived(first.at[1], first_recv.at[1])
     for q in range(half):
@@ -256,11 +284,9 @@
     wide_rows[0:CAND, COLS:2 * COLS] = blank
     wide_rows[CAND:2 * CAND, 0:COLS] = blank
     wide_rows[CAND:2 * CAND, COLS:2 * COLS] = rows_v[...]
-    for v in (xl, xr, xo):
-        arrived(lab_sum.at[v], sum_recv.at[v])
-    rest = jnp.zeros((ROWS, 2 * CAND), F32)
-    for v in range(NX):
-        rest += lab_sum[v].astype(F32)
+    for v in line:
+        arrived(lab_all.at[v], all_recv.at[v])
+    rest = lab_all[...].reshape(ROWS, 2 * CAND)
     terms = []
     for _ in range(3):
         term = rest.astype(BF16)
@@ -290,11 +316,15 @@
         ]
 
     def forwards(q):
-        order = [zl] + line
-        return [
-            out_copy(q, v * NX + (xl if m < 2 else xr), 11 + m, right if m < 2 else left)
-            for m, v in enumerate(order)
-        ]
+        swap = q % 2 == 1
+        copies = []
+        for m, v in enumerate([zl] + line):
+            copies.append((
+                jnp.logical_xor(swap, m < 2),
+                out_copy(q, v * NX + xl, 11 + m, right),
+                out_copy(q, v * NX + xr, 11 + m, left),
+            ))
+        return copies
 
     def out_arrived(q, index):
         arrived(wout.at[index, pl.ds(q * STEP, STEP)], out_recv.at[q, index])
@@ -347,11 +377,16 @@
             line_sends(q)[2 * m + 1].start()
 
     def pass_ring(q):
-        copies = forwards(q)
-        for m, v in enumerate([zl] + line):
-            out_arrived(q, v * NX + xl)
-            out_arrived(q, v * NX + xr)
-            copies[m].start()
+        for (rightward, to_right, to_left), v in zip(forwards(q), [zl] + line):
+            @pl.when(rightward)
+            def _():
+                out_arrived(q, v * NX + xl)
+                to_right.start()
+
+            @pl.when(jnp.logical_not(rightward))
+            def _():
+                out_arrived(q, v * NX + xr)
+                to_left.start()
 
     def spread_step(t, carry):
         @pl.when(t < PARTS)
@@ -367,9 +402,11 @@
     lax.fori_loop(0, PARTS + 1, spread_step, 0)
 
     def last_step(q, carry):
-        for v in [zl] + line:
+        for (rightward, to_right, to_left), v in zip(forwards(q), [zl] + line):
+            out_arrived(q, v * NX + jnp.where(rightward, xr, xl))
             out_arrived(q, v * NX + xo)
-        for copy in own_sends(q) + line_sends(q) + forwards(q):
+            to_right.wait_send()
+        for copy in own_sends(q) + line_sends(q):
             copy.wait_send()
         for copy in second_copies(q):
             copy.wait_send()
@@ -385,9 +422,9 @@
 
         for n in range(SUB):
             own_copy(1, h, n).wait_send()
-    for copy in hid_copies + labs_copies:
+    for copy in hid_copies:
         copy.wait_send()
-    for copy in sum_copies:
+    for copy in cut_copies + sum_copies + all_copies:
         copy.wait_send()
     for copy in first_copies:
         copy.wait_send()
@@ -455,13 +492,15 @@
             pltpu.VMEM(state, BF16),
             pltpu.VMEM(state, I32),
             pltpu.VMEM((NL, ROWS, TOK), BF16),
-            pltpu.VMEM((NL, 8, TOK), I32),
             pltpu.VMEM((NX, NC, NL, TOK, HALF), BF16),
             pltpu.VMEM((NX, ROWS, COLS), BF16),
             pltpu.VMEM(state, F32),
             pltpu.VMEM((2, TOP, COLS), BF16),
             pltpu.VMEM((2, ROWS, COLS), BF16),
-            pltpu.VMEM((NX, ROWS, 2 * CAND), BF16),
+            pltpu.VMEM((NL, STEP, 2 * CAND), BF16),
+            pltpu.VMEM((NL, STEP, 2 * CAND), BF16),
+            pltpu.VMEM((NX, STEP, 2 * CAND), F32),
+            pltpu.VMEM((NL, STEP, 2 * CAND), F32),
             pltpu.VMEM((2 * CAND, 2 * COLS), BF16),
             pltpu.VMEM((ROWS, 2 * COLS), F32),
             dma((9,)),
@@ -474,8 +513,10 @@
             dma((NL,)),
             dma((NL - 1,)),
             dma((NL,)),
-            dma((3,)),
+            dma((NX - 1,)),
             dma((NX,)),
+            dma((NL - 1,)),
+            dma((NL,)),
             dma((2,)),
             dma((2,)),
             dma((2, PARTS)),

time: 101 us -> 95.3 us (0.944)
  the two profiles are of different devices: /device:TPU:64 before, /device:TPU:8 now
where the time goes in v3:
time: 95.3 us; the launch traced here: 95.2 us
  Pallas kernels  94.5 us (99%)
    pallas_call x1, Pallas kernels, on_device(): pl.pallas_call(step_kernel, out_shape=[pltpu.VMEM((groups, ROWS, COLS), B...  92.4 us
    pallas_call x1, Pallas kernels, on_device(): pl.pallas_call(place_kernel, out_shape=[jax.ShapeDtypeStruct((ROWS, group...  2.13 us

profile of v3, /device:TPU:8, one launch (start us, length us, event | category | flops | bytes accessed | tf_op | source)
XLA Modules:
  0.0 95.2 jit_solution(8495574000591092277)
XLA Ops:
  0.6 92.4 %sophia_step.1 = (bf16[16,448,256]{2,1,0:T(8,128)(2,1)S(1)}, bf16[448,256]{1,0:T(8,128)(2,1)S(1)}, bf16[448,256]{1,0:T(8,128)(2,1)S(1)}) custom-call(bf16[2,448,256]{2,1,0:T(8,128)(2,1)} %bitcast.3, bf16[256,128]{1,0:T(8,128)(2,1)} %cot_in.1, bf16[64,256]{1,0:T(8,128)(2,1)} %rows_in.1, s32[1,256]{1,0:T(1,128)} %bitcast.4, s32[1,256]{1,0:T(1,128)} %bitcast.5, ...), custom_call_target="tpu_custom_call" | custom-call | flops 1000000000 | bytes 6000000 | tf_op jit(solution)/shard_map/sophia_step/pallas_call | solution.py:475
  93.0 2.1 %place.1 = (bf16[448,4096]{1,0:T(8,128)(2,1)}, bf16[448,256]{1,0:T(8,128)(2,1)}, bf16[448,256]{1,0:T(8,128)(2,1)}) custom-call(bf16[16,448,256]{2,1,0:T(8,128)(2,1)S(1)} %get-tuple-element.6.wide, bf16[448,256]{1,0:T(8,128)(2,1)S(1)} %get-tuple-element.7.moment, bf16[448,256]{1,0:T(8,128)(2,1)S(1)} %get-tuple-element.8.curv), custom_call_target="tpu_custom_call" | custom-call | tf_op jit(solution)/shard_map/place/pallas_call | solution.py:539

commit v4 on v3

--- a/solution.py
+++ b/solution.py
@@ -18,7 +18,7 @@
 ROWS, TOK, COLS, HALF, CAND = 448, 256, 256, 128, 64
 PARTS = 4
 SUB, LAG = 1, 3
-HID_AT, CUT_AT = 4, 11
+HID_AT, CUT_AT = 5, 14
 BLOCKS = NZ * SUB
 FINE = TOK // SUB
 STEP = ROWS // PARTS
@@ -399,20 +399,12 @@
 
         return carry
 
-    lax.fori_loop(0, PARTS + 1, spread_step, 0)
-
-    def last_step(q, carry):
-        for (rightward, to_right, to_left), v in zip(forwards(q), [zl] + line):
-            out_arrived(q, v * NX + jnp.where(rightward, xr, xl))
-            out_arrived(q, v * NX + xo)
-            to_right.wait_send()
-        for copy in own_sends(q) + line_sends(q):
-            copy.wait_send()
+    def second_drain(q, carry):
         for copy in second_copies(q):
             copy.wait_send()
         return carry
 
-    lax.fori_loop(0, PARTS, last_step, 0)
+    lax.fori_loop(0, PARTS, second_drain, 0)
 
     for h in range(NH):
         @pl.when(jnp.logical_or(zl != row, zh != h))
@@ -446,6 +438,20 @@
         return carry
 
     lax.fori_loop(0, BLOCKS, drain_chain, 0)
+
+    lax.fori_loop(0, PARTS + 1, spread_step, 0)
+
+    def last_step(q, carry):
+        for (rightward, to_right, to_left), v in zip(forwards(q), [zl] + line):
+            to_right.wait_send()
+        for copy in own_sends(q) + line_sends(q):
+            copy.wait_send()
+        for (rightward, to_right, to_left), v in zip(forwards(q), [zl] + line):
+            out_arrived(q, v * NX + jnp.where(rightward, xr, xl))
+            out_arrived(q, v * NX + xo)
+        return carry
+
+    lax.fori_loop(0, PARTS, last_step, 0)
 
 
 def place_kernel(wide, moment, curv, wide_out, moment_out, curv_out, sem):

time: 95.3 us -> 95.1 us (level)
  the two profiles are of different devices: /device:TPU:8 before, /device:TPU:16 now
where the time goes in v4:
time: 95.1 us; the launch traced here: 94.9 us
  Pallas kernels  94.3 us (99%)
    pallas_call x1, Pallas kernels, on_device(): pl.pallas_call(step_kernel, out_shape=[pltpu.VMEM((groups, ROWS, COLS), B...  92.2 us
    pallas_call x1, Pallas kernels, on_device(): pl.pallas_call(place_kernel, out_shape=[jax.ShapeDtypeStruct((ROWS, group...  2.13 us

profile of v4, /device:TPU:16, one launch (start us, length us, event | category | flops | bytes accessed | tf_op | source)
XLA Modules:
  0.0 94.9 jit_solution(16043530094196216207)
XLA Ops:
  0.6 92.2 %sophia_step.1 = (bf16[16,448,256]{2,1,0:T(8,128)(2,1)S(1)}, bf16[448,256]{1,0:T(8,128)(2,1)S(1)}, bf16[448,256]{1,0:T(8,128)(2,1)S(1)}) custom-call(bf16[2,448,256]{2,1,0:T(8,128)(2,1)} %bitcast.3, bf16[256,128]{1,0:T(8,128)(2,1)} %cot_in.1, bf16[64,256]{1,0:T(8,128)(2,1)} %rows_in.1, s32[1,256]{1,0:T(1,128)} %bitcast.4, s32[1,256]{1,0:T(1,128)} %bitcast.5, ...), custom_call_target="tpu_custom_call" | custom-call | flops 1000000000 | bytes 6000000 | tf_op jit(solution)/shard_map/sophia_step/pallas_call | solution.py:481
  92.8 2.1 %place.1 = (bf16[448,4096]{1,0:T(8,128)(2,1)}, bf16[448,256]{1,0:T(8,128)(2,1)}, bf16[448,256]{1,0:T(8,128)(2,1)}) custom-call(bf16[16,448,256]{2,1,0:T(8,128)(2,1)S(1)} %get-tuple-element.6.wide, bf16[448,256]{1,0:T(8,128)(2,1)S(1)} %get-tuple-element.7.moment, bf16[448,256]{1,0:T(8,128)(2,1)S(1)} %get-tuple-element.8.curv), custom_call_target="tpu_custom_call" | custom-call | tf_op jit(solution)/shard_map/place/pallas_call | solution.py:545
